TPU v7x, 128 devices: a whole 4x4x4 slice. The times are simulated.
128 devices in a mesh: segment: 4 (over y), hid: 32 (over z, x, core).
Axes of the slice: x: 4, y: 4, z: 4, core: 2. Of those that a mesh axis runs over, the one named last changes fastest.
Arguments:
- tokens: bfloat16 [4, 128, 8192], P(None, None, 'hid'), may hold values from -34 to 34
- cotangent: bfloat16 [4, 128, 8192], P(None, None, 'hid'), may hold values from -0.70710678 to 0.70710678
- gain: float32 [4, 8192], P('segment', 'hid'), may hold values from 0.1 to 1.9
- weight_in: bfloat16 [4, 64, 128, 512], P('segment', 'hid'), may hold values from -0.35355339 to 0.3723034
- weight_mid: bfloat16 [4, 256, 128, 128], P('segment', 'hid'), may hold values from -0.35355339 to 0.3660534
- weight_low: bfloat16 [4, 256, 128, 128], P('segment', 'hid'), may hold values from -0.35355339 to 0.3660534
- weight_out: bfloat16 [4, 64, 512, 128], P('segment', 'hid'), may hold values from -0.176776695 to 0.1814642
- order_up: int32 [4, 128], P('segment'), may hold values from 0 to 127, each once within a row
- order_down: int32 [4, 128], P('segment'), may hold values from 0 to 127, each once within a row
Outputs:
- grad_in: float32 [4, 64, 128, 512], P('segment', 'hid')
- grad_mid: float32 [4, 256, 128, 128], P('segment', 'hid')
- grad_low: float32 [4, 256, 128, 128], P('segment', 'hid')
- grad_out: float32 [4, 64, 512, 128], P('segment', 'hid')
- grad_gain: float32 [4, 8192], P('segment', 'hid')
Inputs may be any that keep to these rules, and one draw needn't show every extreme that they name: `order_up`: each row holds every number of 0 to 127 once. `order_down`: each row holds every number of 0 to 127 once.
All inputs are finite; a program needn't handle non-finite values.
Results may differ from a plain program's by a relative error of at most 0.024.
Values may be sent and summed in bfloat16 or wider, within the bound.
A program may use at most 64 MiB of HBM per device.

v0:
```python
import jax
import jax.numpy as jnp
from jax import lax
from jax.sharding import PartitionSpec as P

D = 8192
FF = 32768
BLK = 128


epsilon = 1e-05
root_two_pi = 0.7978845608028654
cubic = 0.044715


def from_behind(value, axis, steps):
    count = lax.axis_size(axis)
    first, last = (max(0, -steps), min(count, count - steps))
    return lax.ppermute(value, axis, [(source, source + steps) for source in range(first, last)])


def gelu_pair(pre_act):
    inner_arg = root_two_pi * (pre_act + cubic * pre_act * pre_act * pre_act)
    tangent = jnp.tanh(inner_arg)
    gelu_value = 0.5 * pre_act * (1.0 + tangent)
    gelu_slope = 0.5 * (1.0 + tangent) + 0.5 * pre_act * (1.0 - tangent * tangent) * root_two_pi * (
        1.0 + 3.0 * cubic * pre_act * pre_act
    )
    return (gelu_value, gelu_slope)


def row_total(partial_rows):
    return lax.psum(partial_rows, "hid")


def to_columns(flat_rows):
    group_size = lax.axis_size("hid")
    count_rows = flat_rows.shape[0]
    lanes_local = BLK // group_size
    blocks_local = FF // BLK // group_size
    arranged = jnp.transpose(
        flat_rows.reshape(count_rows, lanes_local, group_size, blocks_local), (2, 1, 3, 0)
    )
    received = lax.all_to_all(arranged, "hid", split_axis=0, concat_axis=1, tiled=True)
    return jnp.transpose(received.reshape(BLK, blocks_local, count_rows), (2, 1, 0))


def to_rows(column_rows):
    group_size = lax.axis_size("hid")
    count_rows = column_rows.shape[0]
    blocks_local = column_rows.shape[1]
    lanes_local = BLK // group_size
    arranged = jnp.transpose(column_rows, (2, 1, 0)).reshape(
        group_size, lanes_local, blocks_local, count_rows
    )
    received = lax.all_to_all(arranged, "hid", split_axis=0, concat_axis=2, tiled=True)
    return jnp.transpose(
        received.reshape(lanes_local * blocks_local * group_size, count_rows), (1, 0)
    )


def section_forward(
    rows_in, gain_row, local_in, local_mid, local_low, local_out, up_order, undo_down
):
    count_rows = rows_in.shape[0]
    blocks_in = local_in.shape[0]
    rows_f32 = rows_in.astype(jnp.float32)
    inv_rms = lax.rsqrt(row_total(jnp.sum(rows_f32 * rows_f32, axis=1)) / D + epsilon)[:, None]
    normed = (rows_f32 * inv_rms * gain_row).astype(jnp.bfloat16)
    hidden = jnp.einsum(
        "tbi,bij->tbj",
        normed.reshape(count_rows, blocks_in, BLK),
        local_in,
        preferred_element_type=jnp.float32,
    ).astype(jnp.bfloat16)
    values_in = jnp.take(to_columns(hidden.reshape(count_rows, -1)), up_order, axis=2)
    pre_act = jnp.einsum("tcq,cqk->tck", values_in, local_mid, preferred_element_type=jnp.float32)
    gelu_value, gelu_slope = gelu_pair(pre_act)
    activated = gelu_value.astype(jnp.bfloat16)
    lowered = jnp.einsum(
        "tcq,cqk->tck", activated, local_low, preferred_element_type=jnp.float32
    ).astype(jnp.bfloat16)
    spread = to_rows(jnp.take(lowered, undo_down, axis=2)).reshape(count_rows, blocks_in, -1)
    branch = jnp.einsum(
        "tbj,bji->tbi", spread, local_out, preferred_element_type=jnp.float32
    ).reshape(count_rows, -1)
    rows_out = (rows_f32 + branch).astype(jnp.bfloat16)
    return (rows_out, (inv_rms, normed, values_in, spread))


def section_backward(
    error_in,
    rows_in,
    kept,
    gain_row,
    local_in,
    local_mid,
    local_low,
    local_out,
    down_order,
    undo_up,
):
    inv_rms, normed, values_in, spread = kept
    count_rows = error_in.shape[0]
    blocks_in = local_in.shape[0]
    rows_f32 = rows_in.astype(jnp.float32)
    error_blocks = error_in.reshape(count_rows, blocks_in, BLK)
    grad_out = jnp.einsum("tbj,tbi->bji", spread, error_blocks, preferred_element_type=jnp.float32)
    d_spread = jnp.einsum(
        "tbi,bji->tbj", error_blocks, local_out, preferred_element_type=jnp.float32
    ).astype(jnp.bfloat16)
    d_lowered = jnp.take(to_columns(d_spread.reshape(count_rows, -1)), down_order, axis=2)
    pre_act = jnp.einsum("tcq,cqk->tck", values_in, local_mid, preferred_element_type=jnp.float32)
    gelu_value, gelu_slope = gelu_pair(pre_act)
    activated = gelu_value.astype(jnp.bfloat16)
    grad_low = jnp.einsum("tcq,tck->cqk", activated, d_lowered, preferred_element_type=jnp.float32)
    d_pre = (
        jnp.einsum("tck,cqk->tcq", d_lowered, local_low, preferred_element_type=jnp.float32)
        * gelu_slope
    ).astype(jnp.bfloat16)
    grad_mid = jnp.einsum("tcq,tck->cqk", values_in, d_pre, preferred_element_type=jnp.float32)
    d_values = jnp.einsum(
        "tck,cqk->tcq", d_pre, local_mid, preferred_element_type=jnp.float32
    ).astype(jnp.bfloat16)
    d_hidden = to_rows(jnp.take(d_values, undo_up, axis=2)).reshape(count_rows, blocks_in, -1)
    grad_in = jnp.einsum(
        "tbi,tbj->bij",
        normed.reshape(count_rows, blocks_in, BLK),
        d_hidden,
        preferred_element_type=jnp.float32,
    )
    d_normed = jnp.einsum(
        "tbj,bij->tbi", d_hidden, local_in, preferred_element_type=jnp.float32
    ).reshape(count_rows, -1)
    grad_gain = jnp.sum(d_normed * rows_f32 * inv_rms, axis=0)
    inner_sum = row_total(jnp.sum(d_normed * gain_row * rows_f32, axis=1))[:, None]
    error_out = (
        error_in.astype(jnp.float32)
        + inv_rms * gain_row * d_normed
        - rows_f32 * inv_rms**3 * inner_sum / D
    ).astype(jnp.bfloat16)
    return (error_out, (grad_in, grad_mid, grad_low, grad_out, grad_gain))


def shards(
    tokens, cotangent, gain, weight_in, weight_mid, weight_low, weight_out, order_up, order_down
):
    segment_count = lax.axis_size("segment")
    segment_index = lax.axis_index("segment")
    batches = tokens.shape[0]
    tick_count = batches + segment_count - 1
    gain_row = gain[0]
    local_in = weight_in[0]
    local_mid = weight_mid[0]
    local_low = weight_low[0]
    local_out = weight_out[0]
    up_order = order_up[0]
    down_order = order_down[0]
    undo_up = jnp.argsort(up_order)
    undo_down = jnp.argsort(down_order)
    carried = jnp.zeros_like(tokens[0])
    rows_list = []
    for step_index in range(tick_count):
        entry_rows = jnp.where(segment_index == 0, tokens[min(step_index, batches - 1)], carried)
        rows_out, kept = section_forward(
            entry_rows, gain_row, local_in, local_mid, local_low, local_out, up_order, undo_down
        )
        rows_list.append(entry_rows)
        if step_index + 1 < tick_count:
            carried = from_behind(rows_out, "segment", 1)
    saved_rows = jnp.stack(rows_list)
    flowing = jnp.zeros_like(cotangent[0])
    running = (
        jnp.zeros(local_in.shape, jnp.float32),
        jnp.zeros(local_mid.shape, jnp.float32),
        jnp.zeros(local_low.shape, jnp.float32),
        jnp.zeros(local_out.shape, jnp.float32),
        jnp.zeros(gain_row.shape, jnp.float32),
    )
    for step_index in range(tick_count):
        raw_position = step_index - (segment_count - 1 - segment_index)
        active = (raw_position >= 0) & (raw_position < batches)
        forward_tick = jnp.clip(raw_position + segment_index, 0, tick_count - 1)
        entry_error = jnp.where(
            segment_index == segment_count - 1, cotangent[min(step_index, batches - 1)], flowing
        )
        rows_in = lax.dynamic_index_in_dim(saved_rows, forward_tick, 0, keepdims=False)
        ignored, kept = section_forward(
            rows_in, gain_row, local_in, local_mid, local_low, local_out, up_order, undo_down
        )
        error_out, grads_here = section_backward(
            entry_error,
            rows_in,
            kept,
            gain_row,
            local_in,
            local_mid,
            local_low,
            local_out,
            down_order,
            undo_up,
        )
        running = jax.tree.map(
            lambda total_now, increment: total_now + jnp.where(active, increment, 0.0),
            running,
            grads_here,
        )
        if step_index + 1 < tick_count:
            flowing = from_behind(error_out, "segment", -1)
    return (
        running[0][None],
        running[1][None],
        running[2][None],
        running[3][None],
        running[4][None],
    )


def solution(mesh):
    in_specs = (
        P(None, None, "hid"),
        P(None, None, "hid"),
        P("segment", "hid"),
        P("segment", "hid", None, None),
        P("segment", "hid", None, None),
        P("segment", "hid", None, None),
        P("segment", "hid", None, None),
        P("segment", None),
        P("segment", None),
    )
    out_specs = (
        P("segment", "hid", None, None),
        P("segment", "hid", None, None),
        P("segment", "hid", None, None),
        P("segment", "hid", None, None),
        P("segment", "hid"),
    )
    return jax.shard_map(shards, mesh=mesh, in_specs=in_specs, out_specs=out_specs, check_vma=False)
```

profile of v0, /device:TPU:1, one launch (start us, length us, event | category | flops | bytes accessed | tf_op | source)
XLA Modules:
  0.0 1550.5 jit_solution(1712866625421229259)
XLA Ops:
  1.9 64.8 %psum.133 = f32[128]{0:T(128)S(1)} all-reduce(f32[128]{0:T(128)S(1)} %fusion.372), channel_id=1, replica_groups=mesh['segment'=4,'hid'=32] {'hid'}, use_global_device_ids=true, to_apply=%region_1.2 | all-reduce | flops 128 | bytes 1024 | tf_op jit(solution)/shard_map/psum | solution.py:33
  68.0 8.5 all-to-all-start
  88.1 12.6 all_to_all.480
  105.7 63.1 %psum.134 = f32[128]{0:T(128)S(1)} all-reduce(f32[128]{0:T(128)S(1)} %get-tuple-element.48), channel_id=1, replica_groups=mesh['segment'=4,'hid'=32] {'hid'}, use_global_device_ids=true, to_apply=%region_4.6 | all-reduce | flops 128 | bytes 1024 | tf_op jit(solution)/shard_map/psum | solution.py:33
  169.4 13.6 all_to_all.481
  185.4 12.5 all_to_all.482
  203.7 63.1 %psum.135 = f32[128]{0:T(128)S(1)} all-reduce(f32[128]{0:T(128)S(1)} %get-tuple-element.46), channel_id=1, replica_groups=mesh['segment'=4,'hid'=32] {'hid'}, use_global_device_ids=true, to_apply=%region_6.8 | all-reduce | flops 128 | bytes 1024 | tf_op jit(solution)/shard_map/psum | solution.py:33
  267.5 13.6 all_to_all.483
  283.5 12.5 all_to_all.484
  301.8 63.1 %psum.136 = f32[128]{0:T(128)S(1)} all-reduce(f32[128]{0:T(128)S(1)} %get-tuple-element.44), channel_id=1, replica_groups=mesh['segment'=4,'hid'=32] {'hid'}, use_global_device_ids=true, to_apply=%region_8.10 | all-reduce | flops 128 | bytes 1024 | tf_op jit(solution)/shard_map/psum | solution.py:33
  365.6 13.6 all_to_all.485
  381.6 12.5 all_to_all.486
  399.9 63.1 %psum.137 = f32[128]{0:T(128)S(1)} all-reduce(f32[128]{0:T(128)S(1)} %get-tuple-element.42), channel_id=1, replica_groups=mesh['segment'=4,'hid'=32] {'hid'}, use_global_device_ids=true, to_apply=%region_10.12 | all-reduce | flops 128 | bytes 1024 | tf_op jit(solution)/shard_map/psum | solution.py:33
  470.1 8.7 all-to-all-done.8
  487.2 7.6 all-to-all-done.9
  500.6 63.1 %psum.138 = f32[128]{0:T(128)S(1)} all-reduce(f32[128]{0:T(128)S(1)} %get-tuple-element.40), channel_id=1, replica_groups=mesh['segment'=4,'hid'=32] {'hid'}, use_global_device_ids=true, to_apply=%region_12.14 | all-reduce | flops 128 | bytes 1024 | tf_op jit(solution)/shard_map/psum | solution.py:33
  570.5 9.0 all-to-all-done.10
  586.4 9.0 all-to-all-done.11
  605.7 63.5 %psum.139 = f32[128]{0:T(128)S(1)} all-reduce(f32[128]{0:T(128)S(1)} %get-tuple-element.11), channel_id=1, replica_groups=mesh['segment'=4,'hid'=32] {'hid'}, use_global_device_ids=true, to_apply=%region_14.16 | all-reduce | flops 128 | bytes 1024 | tf_op jit(solution)/shard_map/psum | solution.py:33
  671.8 8.1 all-to-all-start.13
  709.4 62.3 %all-reduce.5 = (f32[128]{0:T(128)S(1)}, f32[128]{0:T(128)S(1)}) all-reduce(f32[128]{0:T(128)S(1)} %get-tuple-element.17, f32[128]{0:T(128)S(1)} %copy-done.109), channel_id=1, replica_groups=mesh['segment'=4,'hid'=32] {'hid'}, use_global_device_ids=true, to_apply=%region_19.21 | all-reduce | flops 256 | bytes 2048 | tf_op jit(solution)/shard_map/psum | solution.py:33
  774.9 6.0 all-to-all-start.16
  783.8 6.1 all-to-all-done.16
  826.4 6.4 all-to-all-done.17
  835.9 62.2 %all-reduce.4 = (f32[128]{0:T(128)S(1)}, f32[128]{0:T(128)S(1)}) all-reduce(f32[128]{0:T(128)S(1)} %get-tuple-element.19, f32[128]{0:T(128)S(1)} %copy-done.108), channel_id=1, replica_groups=mesh['segment'=4,'hid'=32] {'hid'}, use_global_device_ids=true, to_apply=%region_23.25 | all-reduce | flops 256 | bytes 2048 | tf_op jit(solution)/shard_map/psum | solution.py:33
  904.6 6.8 all-to-all-start.19
  951.5 7.9 all-to-all-start.20
  970.7 62.3 %all-reduce.3 = (f32[128]{0:T(128)S(1)}, f32[128]{0:T(128)S(1)}) all-reduce(f32[128]{0:T(128)S(1)} %get-tuple-element.21, f32[128]{0:T(128)S(1)} %copy-done.107), channel_id=1, replica_groups=mesh['segment'=4,'hid'=32] {'hid'}, use_global_device_ids=true, to_apply=%region_27.29 | all-reduce | flops 256 | bytes 2048 | tf_op jit(solution)/shard_map/psum | solution.py:33
  1037.8 6.0 all-to-all-start.22
  1081.9 7.5 all-to-all-start.23
  1102.1 63.0 %all-reduce.2 = (f32[128]{0:T(128)}, f32[128]{0:T(128)}) all-reduce(f32[128]{0:T(128)} %get-tuple-element.23, f32[128]{0:T(128)} %get-tuple-element.15), channel_id=1, replica_groups=mesh['segment'=4,'hid'=32] {'hid'}, use_global_device_ids=true, to_apply=%region_31.33 | all-reduce | flops 256 | bytes 2048 | tf_op jit(solution)/shard_map/psum | solution.py:33
  1173.8 6.7 all-to-all-start.25
  1214.5 6.4 all-to-all-done.26
  1222.8 62.3 %all-reduce.1 = (f32[128]{0:T(128)S(1)}, f32[128]{0:T(128)S(1)}) all-reduce(f32[128]{0:T(128)S(1)} %get-tuple-element.25, f32[128]{0:T(128)S(1)} %copy-done.106), channel_id=1, replica_groups=mesh['segment'=4,'hid'=32] {'hid'}, use_global_device_ids=true, to_apply=%region_35.37 | all-reduce | flops 256 | bytes 2048 | tf_op jit(solution)/shard_map/psum | solution.py:33
  1288.4 6.0 all-to-all-start.28
  1297.2 6.1 all-to-all-done.28
  1334.0 6.5 all-to-all-done.29
  1343.1 62.2 %all-reduce = (f32[128]{0:T(128)S(1)}, f32[128]{0:T(128)S(1)}) all-reduce(f32[128]{0:T(128)S(1)} %get-tuple-element.27, f32[128]{0:T(128)S(1)} %copy-done.105), channel_id=1, replica_groups=mesh['segment'=4,'hid'=32] {'hid'}, use_global_device_ids=true, to_apply=%region_39.41 | all-reduce | flops 256 | bytes 2048 | tf_op jit(solution)/shard_map/psum | solution.py:33
  1408.7 6.1 all-to-all-start.31
  1416.7 7.2 all-to-all-done.31
  1437.3 6.5 all-to-all-start.33
  1444.1 8.7 all-to-all-done.33
  1460.5 5.7 all-to-all-done.35
  1472.6 7.4 all-to-all-done.37
  1487.5 6.0 all-to-all-done.39
  1512.5 6.5 all-to-all-done.38
  1526.3 6.2 all-to-all-done.34
  1539.3 6.7 all-to-all-done.32
  (628 shorter events, 441.9 us)
Async XLA Ops:
  68.0 17.6 %all-to-all-start = ((bf16[32,4,8,128]{3,2,1,0:T(8,128)(2,1)}), bf16[32,4,8,128]{3,2,1,0:T(8,128)(2,1)S(1)}, u32[]{:S(2)}, u32[]{:S(2)}) async-start(bf16[32,4,8,128]{3,2,1,0:T(8,128)(2,1)} %copy.267), calls=%async_computation | async-start | bytes 524288 | tf_op jit(solution)/shard_map/all_to_all | solution.py:44
  76.6 502.8 %copy-start.74 = (s32[1024]{0:T(1024)}, s32[1024]{0:T(1024)S(1)}, u32[]{:S(2)}) copy-start(s32[1024]{0:T(1024)S(1)} %pad_clamp_fusion.3) | copy-start | bytes 12292
  81.7 499.3 %copy-start.75 = (s32[1024]{0:T(1024)}, s32[1024]{0:T(1024)S(1)}, u32[]{:S(2)}) copy-start(s32[1024]{0:T(1024)S(1)} %pad_clamp_fusion.2) | copy-start | bytes 12292
  101.1 4.5 collective-permute-start
  198.3 5.4 collective-permute-start.1
  296.3 5.4 collective-permute-start.2
  394.4 5.4 collective-permute-start.3
  464.3 14.5 all-to-all-start.8
  482.0 12.8 all-to-all-start.9
  495.1 5.4 collective-permute-start.4
  565.0 14.4 all-to-all-start.10
  582.6 12.8 all-to-all-start.11
  595.4 76.4 %all-to-all-start.12 = ((bf16[32,4,8,128]{3,2,1,0:T(8,128)(2,1)}), bf16[32,4,8,128]{3,2,1,0:T(8,128)(2,1)S(1)}, u32[]{:S(2)}, u32[]{:S(2)}) async-start(bf16[32,4,8,128]{3,2,1,0:T(8,128)(2,1)} %copy.318), calls=%async_computation.12 | async-start | bytes 524288 | tf_op jit(solution)/shard_map/all_to_all | solution.py:44
  599.6 5.4 collective-permute-start.5
  670.5 428.9 %copy-start.13 = (f32[1,128,256]{1,2,0:T(8,128)}, f32[1,128,256]{1,2,0:T(8,128)S(1)}, u32[]{:S(2)}) copy-start(f32[1,128,256]{1,2,0:T(8,128)S(1)} %get-tuple-element.53) | copy-start | bytes 393220
  671.8 17.2 %all-to-all-start.13 = ((bf16[32,4,8,128]{3,2,1,0:T(8,128)(2,1)}), bf16[32,4,8,128]{3,2,1,0:T(8,128)(2,1)S(1)}, u32[]{:S(2)}, u32[]{:S(2)}) async-start(bf16[32,4,8,128]{3,2,1,0:T(8,128)(2,1)} %copy.322), calls=%async_computation.13 | async-start | bytes 524288 | tf_op jit(solution)/shard_map/all_to_all | solution.py:44
  695.1 13.3 all-to-all-start.14
  772.3 8.6 collective-permute-start.6
  774.9 15.0 all-to-all-start.16
  789.9 13.5 all-to-all-start.15
  818.7 14.0 all-to-all-start.17
  900.4 11.1 collective-permute-start.7
  904.6 15.9 %all-to-all-start.19 = ((bf16[32,4,8,128]{3,2,1,0:T(8,128)(2,1)}), bf16[32,4,8,128]{3,2,1,0:T(8,128)(2,1)}, u32[]{:S(2)}, u32[]{:S(2)}) async-start(bf16[32,4,8,128]{3,2,1,0:T(8,128)(2,1)} %copy.348), calls=%async_computation.19 | async-start | bytes 524288 | tf_op jit(solution)/shard_map/all_to_all | solution.py:44
  920.5 15.4 all-to-all-start.18
  951.5 16.7 %all-to-all-start.20 = ((bf16[32,4,8,128]{3,2,1,0:T(8,128)(2,1)}), bf16[32,4,8,128]{3,2,1,0:T(8,128)(2,1)}, u32[]{:S(2)}, u32[]{:S(2)}) async-start(bf16[32,4,8,128]{3,2,1,0:T(8,128)(2,1)} %bitcast.1233), calls=%async_computation.20 | async-start | bytes 524288 | tf_op jit(solution)/shard_map/all_to_all | solution.py:56
  1033.6 10.3 collective-permute-start.8
  1037.8 15.0 all-to-all-start.22
  1052.9 13.5 all-to-all-start.21
  1081.9 16.5 %all-to-all-start.23 = ((bf16[32,4,8,128]{3,2,1,0:T(8,128)(2,1)}), bf16[32,4,8,128]{3,2,1,0:T(8,128)(2,1)}, u32[]{:S(2)}, u32[]{:S(2)}) async-start(bf16[32,4,8,128]{3,2,1,0:T(8,128)(2,1)} %bitcast.1234), calls=%async_computation.23 | async-start | bytes 524288 | tf_op jit(solution)/shard_map/all_to_all | solution.py:56
  1167.9 14.5 collective-permute-start.9
  1173.8 15.8 %all-to-all-start.25 = ((bf16[32,4,8,128]{3,2,1,0:T(8,128)(2,1)}), bf16[32,4,8,128]{3,2,1,0:T(8,128)(2,1)}, u32[]{:S(2)}, u32[]{:S(2)}) async-start(bf16[32,4,8,128]{3,2,1,0:T(8,128)(2,1)} %copy.373), calls=%async_computation.25 | async-start | bytes 524288 | tf_op jit(solution)/shard_map/all_to_all | solution.py:44
  1189.6 12.8 all-to-all-start.24
  1207.3 13.7 all-to-all-start.26
  1285.8 8.6 collective-permute-start.10
  1288.4 15.0 all-to-all-start.28
  1303.3 13.5 all-to-all-start.27
  1327.4 13.1 all-to-all-start.29
  1406.1 8.7 collective-permute-start.11
  1408.7 15.1 all-to-all-start.31
  1423.8 13.5 all-to-all-start.30
  1437.3 15.5 all-to-all-start.33
  1452.8 13.5 all-to-all-start.35
  1466.2 13.7 all-to-all-start.37
  1480.0 13.5 all-to-all-start.39
  1493.5 12.8 all-to-all-start.36
  1506.2 12.8 all-to-all-start.38
  1519.0 13.5 all-to-all-start.34
  1532.5 13.5 all-to-all-start.32
  (113 other events, 1610.9 us)
where the time goes:
time: 1570 us; the launch traced here: 1550 us
  blocking collectives  909 us (58%)
  starting transfers between devices  204 us (13%)
  waiting for transfers between devices  181 us (12%)
  local copies, waits for them, and re-layouts  135 us (9%)
  matrix products  71.2 us (5%)
  other arithmetic  46.2 us (3%)
    psum x13, blocking collectives, row_total(): return lax.psum(partial_rows, 'hid')  818 us
    all_to_all x16, waiting for transfers between devices, to_rows(): lax.all_to_all(arranged, 'hid', split_axis=0, concat_axis=2, tiled=True)  104 us
    all_to_all x17, starting transfers between devices, to_columns(): lax.all_to_all(arranged, 'hid', split_axis=0, concat_axis=1, tiled=True)  94.7 us
    all_to_all x16, starting transfers between devices, to_rows(): lax.all_to_all(arranged, 'hid', split_axis=0, concat_axis=2, tiled=True)  77.9 us
    all_to_all x17, waiting for transfers between devices, to_columns(): lax.all_to_all(arranged, 'hid', split_axis=0, concat_axis=1, tiled=True)  70.9 us
    all_to_all x4, blocking collectives, to_rows(): lax.all_to_all(arranged, 'hid', split_axis=0, concat_axis=2, tiled=True)  50 us
    all_to_all x3, blocking collectives, to_columns(): lax.all_to_all(arranged, 'hid', split_axis=0, concat_axis=1, tiled=True)  40.7 us
    ppermute x12, starting transfers between devices, from_behind(): lax.ppermute(value, axis, [(source, source + steps) for source in range(f...  31.5 us
  transfers between devices with their start and end apart: 45, of which 36 were waited for; matrix products, arithmetic and copies ran while one was open for 8% of the time, Pallas kernels for 0%

commit v1 on v0

v1 whole, which is shorter than its diff:
```python
import functools

import jax
import jax.numpy as jnp
from jax import lax
from jax.experimental import pallas as pl
from jax.experimental.pallas import tpu as pltpu
from jax.sharding import PartitionSpec as P

MESH = pl.DeviceIdType.MESH
BF = jnp.bfloat16
F32 = jnp.float32

D = 8192
SEC = 4
PEERS = 32
LN = 128
epsilon = 1e-05
root_two_pi = 0.7978845608028654
cubic = 0.044715


def mm(left, right):
    return jnp.dot(left, right, preferred_element_type=F32)


def mm_nt(left, right):
    return lax.dot_general(left, right, (((1,), (1,)), ((), ())), preferred_element_type=F32)


def gelu_pair(u):
    inner = root_two_pi * (u + cubic * u * u * u)
    tangent = jnp.tanh(inner)
    value = 0.5 * u * (1.0 + tangent)
    slope = 0.5 * (1.0 + tangent) + 0.5 * u * (1.0 - tangent * tangent) * root_two_pi * (
        1.0 + 3.0 * cubic * u * u
    )
    return value, slope


def iota(shape, dim):
    return lax.broadcasted_iota(jnp.int32, shape, dim)


def kernel(
    tok, cot, small, win, wmid, wlow, wout,
    o_in, o_mid, o_low, o_out, o_gain,
    w_i, w_m, w_l, w_o, sm,
    t_i, t_m, t_l, t_o,
    sel_u, sel_ut, sel_d, sel_dt, g_t,
    perm, perm_t, eye,
    xs, xg, part, parts, r_s, hn,
    s_a, r_a, s_b, r_b,
    v_n, u_s, sl, a_s, g_n, zq, dz, du, e_c, sum_u,
    gs_i, gs_m, gs_l, gs_o, gs_g,
    gr_i, gr_m, gr_l, gr_o, gr_g,
    w_send, w_recv, p_send, p_recv, a_send, a_recv, b_send, b_recv, g_send, g_recv,
):
    me = lax.axis_index("hid")
    seg = lax.axis_index("segment")

    barrier = pltpu.get_barrier_semaphore()

    def greet(k, carry):
        pl.semaphore_signal(
            barrier, inc=1, device_id=(seg, lax.rem(me + k, PEERS)), device_id_type=MESH
        )
        return carry

    lax.fori_loop(1, PEERS, greet, 0)
    for k in range(1, SEC):
        pl.semaphore_signal(
            barrier, inc=1, device_id=(lax.rem(seg + k, SEC), me), device_id_type=MESH
        )
    pl.semaphore_wait(barrier, PEERS - 1 + SEC - 1)

    shared = ((small, sm), (win, w_i), (wmid, w_m), (wlow, w_l), (wout, w_o))

    def broadcast_weights():
        for n, (src, dst) in enumerate(shared):
            pltpu.make_async_copy(src, dst.at[seg], w_recv.at[seg, n]).start()
            for k in (1, 3, 2):
                pltpu.make_async_remote_copy(
                    src, dst.at[seg], w_send.at[n, k - 1], w_recv.at[seg, n],
                    device_id=(lax.rem(seg + k, SEC), me), device_id_type=MESH,
                ).start()

    def wait_weights(s):
        for n, (_, dst) in enumerate(shared):
            pltpu.make_async_copy(dst.at[s], dst.at[s], w_recv.at[s, n]).wait()

    @pl.when(seg == 0)
    def _():
        broadcast_weights()

    u256, n256 = iota((256, 256), 0), iota((256, 256), 1)
    perm[...] = jnp.where(n256 == (u256 % 4) * 64 + u256 // 4, 1.0, 0.0).astype(BF)
    perm_t[...] = jnp.where(u256 == (n256 % 4) * 64 + n256 // 4, 1.0, 0.0).astype(BF)
    eye[...] = jnp.where(iota((LN, LN), 0) == iota((LN, LN), 1), 1.0, 0.0).astype(BF)

    def prepare(s):
        g_t[s] = jnp.transpose(jnp.broadcast_to(sm[s, 0:1, :], (LN, 256)))
        for which, (sel, sel_t) in enumerate(((sel_u, sel_ut), (sel_d, sel_dt))):
            order_row = sm[s, 1:2, which * LN : (which + 1) * LN].astype(jnp.int32)
            order_flat = jnp.broadcast_to(order_row, (512, LN))
            order_col = jnp.transpose(
                jnp.broadcast_to(sm[s, 1:2, which * LN : (which + 1) * LN], (512, LN))
            ).astype(jnp.int32)
            v0 = iota((512, LN), 0)
            v1 = iota((LN, 512), 1)
            for c in range(4):
                hit_t = (order_flat == (v0 // 16) * 4 + v0 % 4) & ((v0 // 4) % 4 == c)
                sel_t[s, :, c * LN : (c + 1) * LN] = jnp.where(hit_t, 1.0, 0.0).astype(BF)
                hit = (order_col == (v1 // 16) * 4 + v1 % 4) & ((v1 // 4) % 4 == c)
                sel[s, c * LN : (c + 1) * LN, :] = jnp.where(hit, 1.0, 0.0).astype(BF)
        ident = eye[...]
        for b in range(2):
            for m in range(4):
                t_i[s, b, m * LN : (m + 1) * LN, :] = mm_nt(
                    ident, w_i[s, b, :, m * LN : (m + 1) * LN]
                ).astype(BF)
            t_o[s, b] = mm_nt(ident, w_o[s, b]).astype(BF)
        for c in range(8):
            t_m[s, c] = mm_nt(ident, w_m[s, c]).astype(BF)
            t_l[s, c] = mm_nt(ident, w_l[s, c]).astype(BF)

    def send_part(way, s):
        def one(k, carry):
            pltpu.make_async_remote_copy(
                part.at[way, s], parts.at[way, s, me], p_send.at[way, s], p_recv.at[way, s],
                device_id=(seg, lax.rem(me + k, PEERS)), device_id_type=MESH,
            ).start()
            return carry

        lax.fori_loop(1, PEERS, one, 0)
        pltpu.make_async_copy(part.at[way, s], parts.at[way, s, me], p_recv.at[way, s]).start()

    def wait_part(way, s):
        whole = parts.at[way, s]
        pltpu.make_async_copy(whole, whole, p_recv.at[way, s]).wait()
        return jnp.sum(parts[way, s].reshape(PEERS, LN), axis=0, keepdims=True)

    def send_a(way, s):
        def one(k, carry):
            to = lax.rem(me + k, PEERS)
            pltpu.make_async_remote_copy(
                s_a.at[way, s, to], r_a.at[way, s, :, me], a_send.at[way, s], a_recv.at[way, s],
                device_id=(seg, to), device_id_type=MESH,
            ).start()
            return carry

        lax.fori_loop(1, PEERS, one, 0)
        pltpu.make_async_copy(
            s_a.at[way, s, me], r_a.at[way, s, :, me], a_recv.at[way, s]
        ).start()

    def send_b(way, s):
        def one(k, carry):
            to = lax.rem(me + k, PEERS)
            pltpu.make_async_remote_copy(
                s_b.at[way, s, :, to], r_b.at[way, s, me], b_send.at[way, s], b_recv.at[way, s],
                device_id=(seg, to), device_id_type=MESH,
            ).start()
            return carry

        lax.fori_loop(1, PEERS, one, 0)
        pltpu.make_async_copy(
            s_b.at[way, s, :, me], r_b.at[way, s, me], b_recv.at[way, s]
        ).start()

    def wait_whole(ref, sem):
        pltpu.make_async_copy(ref, ref, sem).wait()

    def shuffle_out(way, s):
        for m in range(4):
            rows = jnp.concatenate([hn[l, m * 64 : (m + 1) * 64, :] for l in range(4)], axis=0)
            out = mm(perm[...], rows).astype(BF)
            s_a[way, s, m * 8 : (m + 1) * 8] = out.reshape(8, 2, 16, LN)

    def shuffle_in(way, s, store):
        for m in range(4):
            rows = r_b[way, s, m * 8 : (m + 1) * 8].reshape(256, LN)
            out = mm(perm_t[...], rows).astype(BF)
            for l in range(4):
                store(l, m, out[l * 64 : (l + 1) * 64])

    def forward(s, carry):
        wait_weights(s)

        @pl.when(seg == s + 1)
        def _():
            broadcast_weights()

        prepare(s)
        x = xs[s].astype(F32)
        part[0, s] = jnp.sum(x * x, axis=0, keepdims=True)
        send_part(0, s)
        xg[s] = (x * g_t[s]).astype(BF)
        for b in range(2):
            h = mm(t_i[s, b], xg[s, b * LN : (b + 1) * LN]).astype(BF)
            hn[2 * b] = h[:256]
            hn[2 * b + 1] = h[256:]
        shuffle_out(0, s)
        send_a(0, s)
        r = lax.rsqrt(wait_part(0, s) / D + epsilon)
        r_s[s] = r
        wait_whole(r_a.at[0, s], a_recv.at[0, s])
        for q in range(2):
            v = mm(sel_u[s], r_a[0, s, q].reshape(512, LN)).astype(BF)
            v_n[s, q * 4 : (q + 1) * 4] = v.reshape(4, LN, LN)
        for c in range(8):
            u = mm(t_m[s, c], v_n[s, c]) * r
            value, slope = gelu_pair(u)
            a = value.astype(BF)
            u_s[s, c] = u
            sl[s, c] = slope
            a_s[s, c] = a
            zq[c] = mm(t_l[s, c], a).astype(BF)
        for q in range(2):
            z = mm(sel_dt[s], zq[q * 4 : (q + 1) * 4].reshape(512, LN)).astype(BF)
            s_b[0, s, q] = z.reshape(PEERS, 16, LN)
        send_b(0, s)
        wait_whole(r_b.at[0, s], b_recv.at[0, s])

        def store(l, m, value):
            g_n[s, l, m * 64 : (m + 1) * 64, :] = value

        shuffle_in(0, s, store)

        @pl.when(s < SEC - 1)
        def _():
            for b in range(2):
                y = mm(t_o[s, b], g_n[s, 2 * b : 2 * b + 2].reshape(512, LN))
                xs[s + 1, b * LN : (b + 1) * LN] = (
                    xs[s, b * LN : (b + 1) * LN].astype(F32) + y
                ).astype(BF)

        return carry

    xs[0] = jnp.transpose(tok[seg].astype(F32)).astype(BF)
    e_c[...] = jnp.transpose(cot[seg].astype(F32))
    lax.fori_loop(0, SEC, forward, 0)

    grads = ((gs_i, gr_i), (gs_m, gr_m), (gs_l, gr_l), (gs_o, gr_o), (gs_g, gr_g))

    def ship(s, n):
        src, dst = grads[n]

        @pl.when(seg != s)
        def _():
            slot = lax.rem(seg - s + SEC - 1, SEC)
            pltpu.make_async_remote_copy(
                src.at[s], dst.at[slot], g_send.at[s, n], g_recv.at[slot, n],
                device_id=(s, me), device_id_type=MESH,
            ).start()

    def backward(i, carry):
        s = SEC - 1 - i
        own = seg == s

        def emit(out_ref, send_ref, index, value):
            @pl.when(own)
            def _():
                out_ref[index] = value

            @pl.when(jnp.logical_not(own))
            def _():
                send_ref[(s, *index)] = value.astype(BF)

        e16 = e_c[...].astype(BF)
        for b in range(2):
            dg = mm(w_o[s, b], e16[b * LN : (b + 1) * LN]).astype(BF)
            hn[2 * b] = dg[:256]
            hn[2 * b + 1] = dg[256:]
        shuffle_out(1, s)
        send_a(1, s)
        for b in range(2):
            emit(
                o_out, gs_o, (b,),
                mm_nt(g_n[s, 2 * b : 2 * b + 2].reshape(512, LN), e16[b * LN : (b + 1) * LN]),
            )
        ship(s, 3)
        r = r_s[s]
        wait_whole(r_a.at[1, s], a_recv.at[1, s])
        for q in range(2):
            d = mm(sel_d[s], r_a[1, s, q].reshape(512, LN)).astype(BF)
            dz[q * 4 : (q + 1) * 4] = d.reshape(4, LN, LN)
        sum_u[...] = jnp.zeros_like(sum_u)
        for c in range(8):
            d_pre = mm(w_l[s, c], dz[c]) * sl[s, c]
            sum_u[...] += jnp.sum(d_pre * u_s[s, c], axis=0, keepdims=True)
            du[c] = (d_pre * r).astype(BF)
            zq[c] = mm(w_m[s, c], du[c]).astype(BF)
        part[1, s] = sum_u[...]
        send_part(1, s)
        for q in range(2):
            v = mm(sel_ut[s], zq[q * 4 : (q + 1) * 4].reshape(512, LN)).astype(BF)
            s_b[1, s, q] = v.reshape(PEERS, 16, LN)
        send_b(1, s)
        for c in range(8):
            emit(o_low, gs_l, (c,), mm_nt(a_s[s, c], dz[c]))
            emit(o_mid, gs_m, (c,), mm_nt(v_n[s, c], du[c]))
        ship(s, 2)
        ship(s, 1)
        total = wait_part(1, s)
        wait_whole(r_b.at[1, s], b_recv.at[1, s])

        def store(l, m, value):
            hn[l, m * 64 : (m + 1) * 64, :] = value

        shuffle_in(1, s, store)
        scale = r * r * total / D
        for b in range(2):
            lo = b * LN
            dh = hn[2 * b : 2 * b + 2].reshape(512, LN)
            emit(o_in, gs_i, (b,), mm_nt(xg[s, lo : lo + LN], dh))
            dn = mm(w_i[s, b], dh)
            x = xs[s, lo : lo + LN].astype(F32)
            gain_grad = jnp.sum(jnp.transpose(dn * x), axis=0, keepdims=True)

            @pl.when(own)
            def _():
                o_gain[:, lo : lo + LN] = gain_grad

            @pl.when(jnp.logical_not(own))
            def _():
                gs_g[s, :, lo : lo + LN] = gain_grad

            e_c[lo : lo + LN] = (
                (e_c[lo : lo + LN] + g_t[s, lo : lo + LN] * dn - x * scale).astype(BF).astype(F32)
            )
        ship(s, 0)
        ship(s, 4)
        return carry

    lax.fori_loop(0, SEC, backward, 0)

    outs = (o_in, o_mid, o_low, o_out, o_gain)
    for n in (3, 2, 1, 0, 4):
        _, landed = grads[n]
        for slot in range(SEC - 1):
            wait_whole(landed.at[slot], g_recv.at[slot, n])
        outs[n][...] += (
            landed[0].astype(F32) + landed[1].astype(F32) + landed[2].astype(F32)
        )

    def drain(i, carry):
        way, s = i // SEC, lax.rem(i, SEC)
        wait_whole(parts.at[way, s, pl.ds(0, PEERS - 1)], p_send.at[way, s])
        wait_whole(s_a.at[way, s, pl.ds(0, PEERS - 1)], a_send.at[way, s])
        wait_whole(r_b.at[way, s, pl.ds(0, PEERS - 1)], b_send.at[way, s])
        return carry

    lax.fori_loop(0, 2 * SEC, drain, 0)
    for n, (src, _) in enumerate(shared):
        for k in range(SEC - 1):
            wait_whole(src, w_send.at[n, k])

    def drain_grads(s, carry):
        @pl.when(seg != s)
        def _():
            for n in range(5):
                wait_whole(grads[n][0].at[s], g_send.at[s, n])

        return carry

    lax.fori_loop(0, SEC, drain_grads, 0)


def shards(tokens, cotangent, gain, weight_in, weight_mid, weight_low, weight_out, up, down):
    order = jnp.concatenate([up, down], axis=1).astype(F32)
    small = jnp.concatenate([gain, order, jnp.zeros((6, 256), F32)], axis=0)
    vm = pltpu.VMEM
    dma = pltpu.SemaphoreType.DMA
    scratch = [
        vm((SEC, 2, LN, 512), BF), vm((SEC, 8, LN, LN), BF), vm((SEC, 8, LN, LN), BF),
        vm((SEC, 2, 512, LN), BF), vm((SEC, 8, 256), F32),
        vm((SEC, 2, 512, LN), BF), vm((SEC, 8, LN, LN), BF), vm((SEC, 8, LN, LN), BF),
        vm((SEC, 2, LN, 512), BF),
        vm((SEC, 512, 512), BF), vm((SEC, 512, 512), BF), vm((SEC, 512, 512), BF),
        vm((SEC, 512, 512), BF), vm((SEC, 256, LN), F32),
        vm((256, 256), BF), vm((256, 256), BF), vm((LN, LN), BF),
        vm((SEC, 256, LN), BF), vm((SEC, 256, LN), BF), vm((2, SEC, 1, LN), F32),
        vm((2, SEC, PEERS, 1, LN), F32), vm((SEC, 1, LN), F32), vm((4, 256, LN), BF),
        vm((2, SEC, PEERS, 2, 16, LN), BF), vm((2, SEC, 2, PEERS, 16, LN), BF),
        vm((2, SEC, 2, PEERS, 16, LN), BF), vm((2, SEC, PEERS, 2, 16, LN), BF),
        vm((SEC, 8, LN, LN), BF), vm((SEC, 8, LN, LN), F32), vm((SEC, 8, LN, LN), F32),
        vm((SEC, 8, LN, LN), BF), vm((SEC, 4, 256, LN), BF),
        vm((8, LN, LN), BF), vm((8, LN, LN), BF), vm((8, LN, LN), BF),
        vm((256, LN), F32), vm((1, LN), F32),
        vm((SEC, 2, LN, 512), BF), vm((SEC, 8, LN, LN), BF), vm((SEC, 8, LN, LN), BF),
        vm((SEC, 2, 512, LN), BF), vm((SEC, 1, 256), F32),
        vm((3, 2, LN, 512), BF), vm((3, 8, LN, LN), BF), vm((3, 8, LN, LN), BF),
        vm((3, 2, 512, LN), BF), vm((3, 1, 256), F32),
        dma((5, SEC - 1)), dma((SEC, 5)), dma((2, SEC)), dma((2, SEC)), dma((2, SEC)),
        dma((2, SEC)), dma((2, SEC)), dma((2, SEC)), dma((SEC, 5)), dma((3, 5)),
    ]
    whole = pl.BlockSpec(memory_space=pltpu.VMEM)
    g_in, g_mid, g_low, g_out, g_gain = pl.pallas_call(
        kernel,
        out_shape=[
            jax.ShapeDtypeStruct((2, LN, 512), F32),
            jax.ShapeDtypeStruct((8, LN, LN), F32),
            jax.ShapeDtypeStruct((8, LN, LN), F32),
            jax.ShapeDtypeStruct((2, 512, LN), F32),
            jax.ShapeDtypeStruct((1, 256), F32),
        ],
        in_specs=[whole] * 7,
        out_specs=[whole] * 5,
        scratch_shapes=scratch,
        compiler_params=pltpu.CompilerParams(
            collective_id=0, has_side_effects=True, vmem_limit_bytes=60 << 20
        ),
    )(tokens, cotangent, small, weight_in[0], weight_mid[0], weight_low[0], weight_out[0])
    return g_in[None], g_mid[None], g_low[None], g_out[None], g_gain


def solution(mesh):
    in_specs = (
        P(None, None, "hid"),
        P(None, None, "hid"),
        P("segment", "hid"),
        P("segment", "hid", None, None),
        P("segment", "hid", None, None),
        P("segment", "hid", None, None),
        P("segment", "hid", None, None),
        P("segment", None),
        P("segment", None),
    )
    out_specs = (
        P("segment", "hid", None, None),
        P("segment", "hid", None, None),
        P("segment", "hid", None, None),
        P("segment", "hid", None, None),
        P("segment", "hid"),
    )
    return jax.shard_map(shards, mesh=mesh, in_specs=in_specs, out_specs=out_specs, check_vma=False)
```

time: 1570 us -> 271 us (0.17); the launches traced: 1550 us -> 271 us
  blocking collectives: 909 us -> 0 us
  Pallas kernels: 0 us -> 263 us
  starting transfers between devices: 204 us -> 0 us
  waiting for transfers between devices: 181 us -> 0 us
  local copies, waits for them, and re-layouts: 135 us -> 7.08 us
  matrix products: 71.2 us -> 0 us
  other arithmetic: 46.2 us -> 0.67 us
    psum x13 -> x0, blocking collectives: 818 us -> none  [row_total(): return lax.psum(partial_rows, 'hid')]
    pallas_call x0 -> x1, Pallas kernels: none -> 263 us  [shards(): pl.pallas_call(kernel, out_shape=[jax.ShapeDtypeStruct((2, LN, 512), F32)...]
    all_to_all x33 -> x0, waiting for transfers between devices: 175 us -> none  [the longest x16 104 us: to_rows(): lax.all_to_all(arranged, 'hid', split_axis=0, concat_axis=2, tiled=True)]
    all_to_all x33 -> x0, starting transfers between devices: 173 us -> none  [the longest x17 94.7 us: to_columns(): lax.all_to_all(arranged, 'hid', split_axis=0, concat_axis=1, tiled=True)]
    all_to_all x7 -> x0, blocking collectives: 90.7 us -> none  [the longest x4 50 us: to_rows(): lax.all_to_all(arranged, 'hid', split_axis=0, concat_axis=2, tiled=True)]
    dot_general x95 -> x0, matrix products: 71.2 us -> none  [the longest x7 14.2 us: section_backward(): jnp.einsum('tcq,tck->cqk', activated, d_lowered, preferred_element_type=j...]
    gather x40 -> x0, local copies, waits for them, and re-layouts: 54.5 us -> none  [the longest x13 17.6 us: section_forward(): jnp.take(lowered, undo_down, axis=2)]
    ppermute x12 -> x0, starting transfers between devices: 31.5 us -> none  [from_behind(): lax.ppermute(value, axis, [(source, source + steps) for source in range(f...]
  transfers between devices with their start and end apart: 45 -> 0, of which waited for: 36 -> 0; matrix products, arithmetic and copies ran while one was open for 8% -> 0% of each run, Pallas kernels for 0% -> 0%
where the time goes in v1:
time: 271 us
  Pallas kernels  263 us (97%)
  local copies, waits for them, and re-layouts  7.08 us (3%)
    pallas_call x1, Pallas kernels, shards(): pl.pallas_call(kernel, out_shape=[jax.ShapeDtypeStruct((2, LN, 512), F32)...  263 us
    unnamed x19, local copies, waits for them, and re-layouts  7.01 us

profile of v1, /device:TPU:1, one launch (start us, length us, event | category | flops | bytes accessed | tf_op | source)
XLA Modules:
  0.0 271.1 jit_solution(16392655834761835939)
XLA Ops:
  0.6 0.0 copy-start.5
  0.7 0.0 copy-start.6
  0.7 0.1 pad.2.clone
  0.7 0.6 copy-done.5
  1.3 0.0 copy-done.6
  1.3 0.0 copy-start.4
  1.3 0.7 copy-done.4
  2.0 0.7 maximum_maximum_fusion.small
  2.7 262.7 %shard_map.128 = (f32[2,128,512]{2,1,0:T(8,128)}, f32[8,128,128]{2,1,0:T(8,128)}, f32[8,128,128]{2,1,0:T(8,128)}, f32[2,512,128]{2,1,0:T(8,128)}, f32[1,256]{1,0:T(1,128)}) custom-call(bf16[4,128,256]{2,1,0:T(8,128)(2,1)} %tok.1, bf16[4,128,256]{2,1,0:T(8,128)(2,1)} %cot.1, f32[8,256]{1,0:T(8,128)} %maximum_maximum_fusion.small, ...), custom_call_target="tpu_custom_call" | custom-call | tf_op jit(solution)/shard_map/pallas_call | solution.py:399
  265.4 0.0 copy-start.2
  265.4 1.9 copy.19
  267.3 0.0 copy-done.2
  267.3 0.0 copy-start.1
  267.3 0.8 copy.20
  268.1 0.4 copy-done.1
  268.5 0.0 copy-start
  268.5 0.8 copy.21
  269.3 0.4 copy-done
  269.8 0.0 copy-start.3
  269.8 0.8 copy.22
  270.6 0.0 copy-done.3
  270.6 0.6 copy.23
  (2 shorter events, 0.0 us)
Async XLA Ops:
  0.6 0.7 copy-start.5
  0.7 0.7 copy-start.6
  1.3 0.7 copy-start.4
  265.4 1.9 copy-start.2
  267.3 1.2 copy-start.1
  268.5 1.2 copy-start
  269.8 0.8 copy-start.3

commit v2 on v1

--- a/solution.py
+++ b/solution.py
@@ -53,8 +53,10 @@
     s_a, r_a, s_b, r_b,
     v_n, u_s, sl, a_s, g_n, zq, dz, du, e_c, sum_u,
     gs_i, gs_m, gs_l, gs_o, gs_g,
+    gh_i, gh_m, gh_l, gh_o,
     gr_i, gr_m, gr_l, gr_o, gr_g,
-    w_send, w_recv, p_send, p_recv, a_send, a_recv, b_send, b_recv, g_send, g_recv,
+    w_send, w_recv, w_pass, p_send, p_recv, a_send, a_recv, b_send, b_recv,
+    g_send, g_recv, h_send, h_recv, gg_send, gg_recv,
 ):
     me = lax.axis_index("hid")
     seg = lax.axis_index("segment")
@@ -76,20 +78,38 @@
 
     shared = ((small, sm), (win, w_i), (wmid, w_m), (wlow, w_l), (wout, w_o))
 
+    def row_at(k):
+        return (lax.rem(seg + k, SEC), me)
+
     def broadcast_weights():
         for n, (src, dst) in enumerate(shared):
-            pltpu.make_async_copy(src, dst.at[seg], w_recv.at[seg, n]).start()
-            for k in (1, 3, 2):
+            for k in (1, 3, 2) if n == 0 else (1, 3):
                 pltpu.make_async_remote_copy(
                     src, dst.at[seg], w_send.at[n, k - 1], w_recv.at[seg, n],
-                    device_id=(lax.rem(seg + k, SEC), me), device_id_type=MESH,
+                    device_id=row_at(k), device_id_type=MESH,
                 ).start()
-
-    def wait_weights(s):
-        for n, (_, dst) in enumerate(shared):
-            pltpu.make_async_copy(dst.at[s], dst.at[s], w_recv.at[s, n]).wait()
-
-    @pl.when(seg == 0)
+            pltpu.make_async_copy(src, dst.at[seg], w_recv.at[seg, n]).start()
+
+    def half(ref, s, h):
+        size = ref.shape[1] // 2
+        return ref.at[s, pl.ds(h * size, size)]
+
+    def take(s, n):
+        dst = shared[n][1]
+        wait_whole(dst.at[s], w_recv.at[s, n])
+        if n == 0:
+            return
+        for h, k in enumerate((1, 3)):
+
+            @pl.when(seg == lax.rem(s + k, SEC))
+            def _():
+                piece = half(dst, s, h)
+                pltpu.make_async_remote_copy(
+                    piece, piece, w_pass.at[n, h], w_recv.at[s, n],
+                    device_id=row_at(k), device_id_type=MESH,
+                ).start()
+
+    @pl.when(lax.rem(seg, 2) == 0)
     def _():
         broadcast_weights()
 
@@ -98,7 +118,13 @@
     perm_t[...] = jnp.where(u256 == (n256 % 4) * 64 + n256 // 4, 1.0, 0.0).astype(BF)
     eye[...] = jnp.where(iota((LN, LN), 0) == iota((LN, LN), 1), 1.0, 0.0).astype(BF)
 
-    def prepare(s):
+    def prepare_in(s):
+        ident = eye[...]
+        for b in range(2):
+            for m in range(4):
+                t_i[s, b, m * LN : (m + 1) * LN, :] = mm_nt(
+                    ident, w_i[s, b, :, m * LN : (m + 1) * LN]
+                ).astype(BF)
         g_t[s] = jnp.transpose(jnp.broadcast_to(sm[s, 0:1, :], (LN, 256)))
         for which, (sel, sel_t) in enumerate(((sel_u, sel_ut), (sel_d, sel_dt))):
             order_row = sm[s, 1:2, which * LN : (which + 1) * LN].astype(jnp.int32)
@@ -113,16 +139,17 @@
                 sel_t[s, :, c * LN : (c + 1) * LN] = jnp.where(hit_t, 1.0, 0.0).astype(BF)
                 hit = (order_col == (v1 // 16) * 4 + v1 % 4) & ((v1 // 4) % 4 == c)
                 sel[s, c * LN : (c + 1) * LN, :] = jnp.where(hit, 1.0, 0.0).astype(BF)
+
+    def prepare_mid(s):
         ident = eye[...]
-        for b in range(2):
-            for m in range(4):
-                t_i[s, b, m * LN : (m + 1) * LN, :] = mm_nt(
-                    ident, w_i[s, b, :, m * LN : (m + 1) * LN]
-                ).astype(BF)
-            t_o[s, b] = mm_nt(ident, w_o[s, b]).astype(BF)
         for c in range(8):
             t_m[s, c] = mm_nt(ident, w_m[s, c]).astype(BF)
             t_l[s, c] = mm_nt(ident, w_l[s, c]).astype(BF)
+
+    def prepare_out(s):
+        ident = eye[...]
+        for b in range(2):
+            t_o[s, b] = mm_nt(ident, w_o[s, b]).astype(BF)
 
     def send_part(way, s):
         def one(k, carry):
@@ -184,14 +211,27 @@
             for l in range(4):
                 store(l, m, out[l * 64 : (l + 1) * 64])
 
+    def start_back(s):
+        e16 = e_c[...].astype(BF)
+        for b in range(2):
+            dg = mm(w_o[s, b], e16[b * LN : (b + 1) * LN]).astype(BF)
+            hn[2 * b] = dg[:256]
+            hn[2 * b + 1] = dg[256:]
+        shuffle_out(1, s)
+        send_a(1, s)
+
+    def gather_g(s):
+        wait_whole(r_b.at[0, s], b_recv.at[0, s])
+
+        def store(l, m, value):
+            g_n[s, l, m * 64 : (m + 1) * 64, :] = value
+
+        shuffle_in(0, s, store)
+
     def forward(s, carry):
-        wait_weights(s)
-
-        @pl.when(seg == s + 1)
-        def _():
-            broadcast_weights()
-
-        prepare(s)
+        take(s, 0)
+        take(s, 1)
+        prepare_in(s)
         x = xs[s].astype(F32)
         part[0, s] = jnp.sum(x * x, axis=0, keepdims=True)
         send_part(0, s)
@@ -202,6 +242,20 @@
             hn[2 * b + 1] = h[256:]
         shuffle_out(0, s)
         send_a(0, s)
+        take(s, 2)
+        take(s, 3)
+
+        @pl.when(seg == 2 * s + 1)
+        def _():
+            broadcast_weights()
+
+        prepare_mid(s)
+
+        @pl.when(s == SEC - 1)
+        def _():
+            take(s, 4)
+            start_back(s)
+
         r = lax.rsqrt(wait_part(0, s) / D + epsilon)
         r_s[s] = r
         wait_whole(r_a.at[0, s], a_recv.at[0, s])
@@ -220,15 +274,12 @@
             z = mm(sel_dt[s], zq[q * 4 : (q + 1) * 4].reshape(512, LN)).astype(BF)
             s_b[0, s, q] = z.reshape(PEERS, 16, LN)
         send_b(0, s)
-        wait_whole(r_b.at[0, s], b_recv.at[0, s])
-
-        def store(l, m, value):
-            g_n[s, l, m * 64 : (m + 1) * 64, :] = value
-
-        shuffle_in(0, s, store)
 
         @pl.when(s < SEC - 1)
         def _():
+            take(s, 4)
+            prepare_out(s)
+            gather_g(s)
             for b in range(2):
                 y = mm(t_o[s, b], g_n[s, 2 * b : 2 * b + 2].reshape(512, LN))
                 xs[s + 1, b * LN : (b + 1) * LN] = (
@@ -241,16 +292,57 @@
     e_c[...] = jnp.transpose(cot[seg].astype(F32))
     lax.fori_loop(0, SEC, forward, 0)
 
-    grads = ((gs_i, gr_i), (gs_m, gr_m), (gs_l, gr_l), (gs_o, gr_o), (gs_g, gr_g))
+    grads = (
+        (gs_i, gh_i, gr_i), (gs_m, gh_m, gr_m), (gs_l, gh_l, gr_l), (gs_o, gh_o, gr_o)
+    )
+
+    def near(s, k):
+        return seg == lax.rem(s + k, SEC)
+
+    def ship_half(s, n, k, h):
+        src, _, dst = grads[n]
+        pltpu.make_async_remote_copy(
+            half(src, s, h), half(dst, k // 2, h), g_send.at[k // 2, n, h],
+            g_recv.at[k // 2, n], device_id=row_at(SEC - k), device_id_type=MESH,
+        ).start()
 
     def ship(s, n):
-        src, dst = grads[n]
-
+        src, mid, _ = grads[n]
+
+        @pl.when(near(s, 1))
+        def _():
+            ship_half(s, n, 1, 1)
+
+        @pl.when(near(s, 3))
+        def _():
+            ship_half(s, n, 3, 0)
+
+        @pl.when(near(s, 2))
+        def _():
+            for h, k in enumerate((3, 1)):
+                pltpu.make_async_remote_copy(
+                    half(src, s, h), mid.at[h], h_send.at[n, h], h_recv.at[h, n],
+                    device_id=row_at(k), device_id_type=MESH,
+                ).start()
+
+    def combine(s, n):
+        src, mid, _ = grads[n]
+        size = src.shape[1] // 2
+        for h, k in enumerate((1, 3)):
+
+            @pl.when(near(s, k))
+            def _():
+                wait_whole(mid.at[h], h_recv.at[h, n])
+                rows = pl.ds(h * size, size)
+                src[s, rows] = (src[s, rows].astype(F32) + mid[h].astype(F32)).astype(BF)
+                ship_half(s, n, k, h)
+
+    def ship_gain(s):
         @pl.when(seg != s)
         def _():
             slot = lax.rem(seg - s + SEC - 1, SEC)
             pltpu.make_async_remote_copy(
-                src.at[s], dst.at[slot], g_send.at[s, n], g_recv.at[slot, n],
+                gs_g.at[s], gr_g.at[slot], gg_send.at[s], gg_recv.at[slot],
                 device_id=(s, me), device_id_type=MESH,
             ).start()
 
@@ -268,18 +360,23 @@
                 send_ref[(s, *index)] = value.astype(BF)
 
         e16 = e_c[...].astype(BF)
-        for b in range(2):
-            dg = mm(w_o[s, b], e16[b * LN : (b + 1) * LN]).astype(BF)
-            hn[2 * b] = dg[:256]
-            hn[2 * b + 1] = dg[256:]
-        shuffle_out(1, s)
-        send_a(1, s)
+
+        @pl.when(i == 0)
+        def _():
+            gather_g(s)
+
         for b in range(2):
             emit(
                 o_out, gs_o, (b,),
                 mm_nt(g_n[s, 2 * b : 2 * b + 2].reshape(512, LN), e16[b * LN : (b + 1) * LN]),
             )
         ship(s, 3)
+
+        @pl.when(i > 0)
+        def _():
+            combine(s + 1, 2)
+            combine(s + 1, 1)
+
         r = r_s[s]
         wait_whole(r_a.at[1, s], a_recv.at[1, s])
         for q in range(2):
@@ -302,6 +399,12 @@
             emit(o_mid, gs_m, (c,), mm_nt(v_n[s, c], du[c]))
         ship(s, 2)
         ship(s, 1)
+
+        @pl.when(i > 0)
+        def _():
+            combine(s + 1, 0)
+
+        combine(s, 3)
         total = wait_part(1, s)
         wait_whole(r_b.at[1, s], b_recv.at[1, s])
 
@@ -330,19 +433,28 @@
                 (e_c[lo : lo + LN] + g_t[s, lo : lo + LN] * dn - x * scale).astype(BF).astype(F32)
             )
         ship(s, 0)
-        ship(s, 4)
+        ship_gain(s)
+
+        @pl.when(s > 0)
+        def _():
+            start_back(s - 1)
+
         return carry
 
     lax.fori_loop(0, SEC, backward, 0)
 
-    outs = (o_in, o_mid, o_low, o_out, o_gain)
-    for n in (3, 2, 1, 0, 4):
-        _, landed = grads[n]
-        for slot in range(SEC - 1):
-            wait_whole(landed.at[slot], g_recv.at[slot, n])
-        outs[n][...] += (
-            landed[0].astype(F32) + landed[1].astype(F32) + landed[2].astype(F32)
-        )
+    combine(0, 2)
+    combine(0, 1)
+    combine(0, 0)
+    outs = (o_in, o_mid, o_low, o_out)
+    for n in (3, 2, 1, 0):
+        _, _, landed = grads[n]
+        for side in range(2):
+            wait_whole(landed.at[side], g_recv.at[side, n])
+        outs[n][...] += landed[0].astype(F32) + landed[1].astype(F32)
+    for slot in range(SEC - 1):
+        wait_whole(gr_g.at[slot], gg_recv.at[slot])
+    o_gain[...] += gr_g[0] + gr_g[1] + gr_g[2]
 
     def drain(i, carry):
         way, s = i // SEC, lax.rem(i, SEC)
@@ -352,19 +464,26 @@
         return carry
 
     lax.fori_loop(0, 2 * SEC, drain, 0)
-    for n, (src, _) in enumerate(shared):
-        for k in range(SEC - 1):
+    for n, (src, dst) in enumerate(shared):
+        for k in range(SEC - 1) if n == 0 else (0, 2):
             wait_whole(src, w_send.at[n, k])
-
-    def drain_grads(s, carry):
+        if n > 0:
+            for h in range(2):
+                wait_whole(half(dst, 0, h), w_pass.at[n, h])
+    for n, (_, mid, landed) in enumerate(grads):
+        for h in range(2):
+            wait_whole(mid.at[h], h_send.at[n, h])
+            for side in range(2):
+                wait_whole(half(landed, side, h), g_send.at[side, n, h])
+
+    def drain_gain(s, carry):
         @pl.when(seg != s)
         def _():
-            for n in range(5):
-                wait_whole(grads[n][0].at[s], g_send.at[s, n])
+            wait_whole(gs_g.at[s], gg_send.at[s])
 
         return carry
 
-    lax.fori_loop(0, SEC, drain_grads, 0)
+    lax.fori_loop(0, SEC, drain_gain, 0)
 
 
 def shards(tokens, cotangent, gain, weight_in, weight_mid, weight_low, weight_out, up, down):
@@ -390,10 +509,14 @@
         vm((256, LN), F32), vm((1, LN), F32),
         vm((SEC, 2, LN, 512), BF), vm((SEC, 8, LN, LN), BF), vm((SEC, 8, LN, LN), BF),
         vm((SEC, 2, 512, LN), BF), vm((SEC, 1, 256), F32),
-        vm((3, 2, LN, 512), BF), vm((3, 8, LN, LN), BF), vm((3, 8, LN, LN), BF),
-        vm((3, 2, 512, LN), BF), vm((3, 1, 256), F32),
-        dma((5, SEC - 1)), dma((SEC, 5)), dma((2, SEC)), dma((2, SEC)), dma((2, SEC)),
-        dma((2, SEC)), dma((2, SEC)), dma((2, SEC)), dma((SEC, 5)), dma((3, 5)),
+        vm((2, 1, LN, 512), BF), vm((2, 4, LN, LN), BF), vm((2, 4, LN, LN), BF),
+        vm((2, 1, 512, LN), BF),
+        vm((2, 2, LN, 512), BF), vm((2, 8, LN, LN), BF), vm((2, 8, LN, LN), BF),
+        vm((2, 2, 512, LN), BF), vm((3, 1, 256), F32),
+        dma((5, SEC - 1)), dma((SEC, 5)), dma((5, 2)),
+        dma((2, SEC)), dma((2, SEC)), dma((2, SEC)),
+        dma((2, SEC)), dma((2, SEC)), dma((2, SEC)),
+        dma((2, 4, 2)), dma((2, 4)), dma((4, 2)), dma((2, 4)), dma((SEC,)), dma((3,)),
     ]
     whole = pl.BlockSpec(memory_space=pltpu.VMEM)
     g_in, g_mid, g_low, g_out, g_gain = pl.pallas_call(

time: 271 us -> 219 us (0.81)
  Pallas kernels: 263 us -> 211 us
    pallas_call x1, Pallas kernels: 263 us -> 211 us  [shards(): pl.pallas_call(kernel, out_shape=[jax.ShapeDtypeStruct((2, LN, 512), F32)...]
where the time goes in v2:
time: 219 us
  Pallas kernels  211 us (96%)
  local copies, waits for them, and re-layouts  7.08 us (3%)
    pallas_call x1, Pallas kernels, shards(): pl.pallas_call(kernel, out_shape=[jax.ShapeDtypeStruct((2, LN, 512), F32)...  211 us
    unnamed x19, local copies, waits for them, and re-layouts  7.01 us

profile of v2, /device:TPU:1, one launch (start us, length us, event | category | flops | bytes accessed | tf_op | source)
XLA Modules:
  0.0 219.2 jit_solution(6525235051031105611)
XLA Ops:
  0.6 0.0 copy-start.5
  0.7 0.0 copy-start.6
  0.7 0.1 pad.2.clone
  0.7 0.6 copy-done.5
  1.3 0.0 copy-done.6
  1.3 0.0 copy-start.4
  1.3 0.7 copy-done.4
  2.0 0.7 maximum_maximum_fusion.small
  2.7 210.8 %shard_map.128 = (f32[2,128,512]{2,1,0:T(8,128)}, f32[8,128,128]{2,1,0:T(8,128)}, f32[8,128,128]{2,1,0:T(8,128)}, f32[2,512,128]{2,1,0:T(8,128)}, f32[1,256]{1,0:T(1,128)}) custom-call(bf16[4,128,256]{2,1,0:T(8,128)(2,1)} %tok.1, bf16[4,128,256]{2,1,0:T(8,128)(2,1)} %cot.1, f32[8,256]{1,0:T(8,128)} %maximum_maximum_fusion.small, ...), custom_call_target="tpu_custom_call" | custom-call | tf_op jit(solution)/shard_map/pallas_call | solution.py:522
  213.4 0.0 copy-start.2
  213.4 1.9 copy.19
  215.4 0.0 copy-done.2
  215.4 0.0 copy-start.1
  215.4 0.8 copy.20
  216.2 0.4 copy-done.1
  216.6 0.0 copy-start
  216.6 0.8 copy.21
  217.4 0.4 copy-done
  217.8 0.0 copy-start.3
  217.8 0.8 copy.22
  218.6 0.0 copy-done.3
  218.6 0.6 copy.23
  (2 shorter events, 0.0 us)
Async XLA Ops:
  0.6 0.7 copy-start.5
  0.7 0.7 copy-start.6
  1.3 0.7 copy-start.4
  213.4 1.9 copy-start.2
  215.4 1.2 copy-start.1
  216.6 1.2 copy-start
  217.8 0.8 copy-start.3

commit v3 on v2

--- a/solution.py
+++ b/solution.py
@@ -61,6 +61,9 @@
     me = lax.axis_index("hid")
     seg = lax.axis_index("segment")
 
+    def peer(k):
+        return lax.rem(me + 1 + k, PEERS)
+
     barrier = pltpu.get_barrier_semaphore()
 
     def greet(k, carry):
@@ -81,37 +84,90 @@
     def row_at(k):
         return (lax.rem(seg + k, SEC), me)
 
-    def broadcast_weights():
-        for n, (src, dst) in enumerate(shared):
-            for k in (1, 3, 2) if n == 0 else (1, 3):
-                pltpu.make_async_remote_copy(
-                    src, dst.at[seg], w_send.at[n, k - 1], w_recv.at[seg, n],
-                    device_id=row_at(k), device_id_type=MESH,
-                ).start()
-            pltpu.make_async_copy(src, dst.at[seg], w_recv.at[seg, n]).start()
+    def near(s, k):
+        return seg == lax.rem(s + k, SEC)
 
     def half(ref, s, h):
         size = ref.shape[1] // 2
         return ref.at[s, pl.ds(h * size, size)]
 
-    def take(s, n):
-        dst = shared[n][1]
-        wait_whole(dst.at[s], w_recv.at[s, n])
-        if n == 0:
-            return
-        for h, k in enumerate((1, 3)):
-
-            @pl.when(seg == lax.rem(s + k, SEC))
-            def _():
-                piece = half(dst, s, h)
+    ways = (1, 3)
+
+    def send_weights(s):
+        @pl.when(seg == s)
+        def _():
+            for k in (1, 3, 2):
                 pltpu.make_async_remote_copy(
-                    piece, piece, w_pass.at[n, h], w_recv.at[s, n],
+                    small, sm.at[s], w_send.at[0, k - 1], w_recv.at[s, 0, 0],
                     device_id=row_at(k), device_id_type=MESH,
                 ).start()
-
-    @pl.when(lax.rem(seg, 2) == 0)
-    def _():
-        broadcast_weights()
+            pltpu.make_async_copy(small, sm.at[s], w_recv.at[s, 0, 0]).start()
+            for n in range(1, 5):
+                src, dst = shared[n]
+                if s > 0:
+                    for k in (1, 3, 2):
+                        pltpu.make_async_remote_copy(
+                            src, dst.at[s], w_send.at[n, k - 1], w_recv.at[s, n, 0],
+                            device_id=row_at(k), device_id_type=MESH,
+                        ).start()
+                    pltpu.make_async_copy(src, dst.at[s], w_recv.at[s, n, 0]).start()
+                    continue
+                size = src.shape[0] // 2
+                for h in range(2):
+                    pltpu.make_async_remote_copy(
+                        src.at[pl.ds(h * size, size)], half(dst, s, h), w_send.at[n, h],
+                        w_recv.at[s, n, h], device_id=row_at(ways[h]), device_id_type=MESH,
+                    ).start()
+                for h in range(2):
+                    pltpu.make_async_copy(
+                        src.at[pl.ds(h * size, size)], half(dst, s, h), w_recv.at[s, n, h]
+                    ).start()
+
+    def arrived(s, n, h):
+        wait_whole(half(shared[n][1], s, h), w_recv.at[s, n, h])
+
+    def pass_on(s, n, h, slot):
+        piece = half(shared[n][1], s, h)
+        pltpu.make_async_remote_copy(
+            piece, piece, w_pass.at[n, slot], w_recv.at[s, n, h],
+            device_id=row_at(ways[h]), device_id_type=MESH,
+        ).start()
+
+    def second(s, n):
+        for h in range(2):
+
+            @pl.when(near(s, ways[h]))
+            def _():
+                arrived(s, n, h)
+                pass_on(s, n, h, h)
+
+    def third(s, n):
+        @pl.when(near(s, 2))
+        def _():
+            for h in range(2):
+                arrived(s, n, h)
+                pass_on(s, n, h, 2 + h)
+
+    def final(s, n):
+        if s > 0:
+            wait_whole(shared[n][1].at[s], w_recv.at[s, n, 0])
+            return
+
+        @pl.when(near(s, 0))
+        def _():
+            arrived(s, n, 0)
+            arrived(s, n, 1)
+
+        for h in range(2):
+
+            @pl.when(near(s, ways[1 - h]))
+            def _():
+                arrived(s, n, h)
+
+    def final_small(s):
+        wait_whole(sm.at[s], w_recv.at[s, 0, 0])
+
+    send_weights(0)
 
     u256, n256 = iota((256, 256), 0), iota((256, 256), 1)
     perm[...] = jnp.where(n256 == (u256 % 4) * 64 + u256 // 4, 1.0, 0.0).astype(BF)
@@ -155,11 +211,11 @@
         def one(k, carry):
             pltpu.make_async_remote_copy(
                 part.at[way, s], parts.at[way, s, me], p_send.at[way, s], p_recv.at[way, s],
-                device_id=(seg, lax.rem(me + k, PEERS)), device_id_type=MESH,
+                device_id=(seg, peer(k)), device_id_type=MESH,
             ).start()
             return carry
 
-        lax.fori_loop(1, PEERS, one, 0)
+        lax.fori_loop(0, PEERS - 1, one, 0)
         pltpu.make_async_copy(part.at[way, s], parts.at[way, s, me], p_recv.at[way, s]).start()
 
     def wait_part(way, s):
@@ -168,31 +224,33 @@
         return jnp.sum(parts[way, s].reshape(PEERS, LN), axis=0, keepdims=True)
 
     def send_a(way, s):
+        for q in range(2):
+
+            def one(k, carry):
+                to = peer(k)
+                pltpu.make_async_remote_copy(
+                    s_a.at[way, s, to, q], r_a.at[way, s, q, me], a_send.at[way, s],
+                    a_recv.at[way, s, q], device_id=(seg, to), device_id_type=MESH,
+                ).start()
+                return carry
+
+            lax.fori_loop(0, PEERS - 1, one, 0)
+            pltpu.make_async_copy(
+                s_a.at[way, s, me, q], r_a.at[way, s, q, me], a_recv.at[way, s, q]
+            ).start()
+
+    def send_b(way, s, q):
         def one(k, carry):
-            to = lax.rem(me + k, PEERS)
+            to = peer(k)
             pltpu.make_async_remote_copy(
-                s_a.at[way, s, to], r_a.at[way, s, :, me], a_send.at[way, s], a_recv.at[way, s],
-                device_id=(seg, to), device_id_type=MESH,
+                s_b.at[way, s, q, to], r_b.at[way, s, me, q], b_send.at[way, s],
+                b_recv.at[way, s], device_id=(seg, to), device_id_type=MESH,
             ).start()
             return carry
 
-        lax.fori_loop(1, PEERS, one, 0)
+        lax.fori_loop(0, PEERS - 1, one, 0)
         pltpu.make_async_copy(
-            s_a.at[way, s, me], r_a.at[way, s, :, me], a_recv.at[way, s]
-        ).start()
-
-    def send_b(way, s):
-        def one(k, carry):
-            to = lax.rem(me + k, PEERS)
-            pltpu.make_async_remote_copy(
-                s_b.at[way, s, :, to], r_b.at[way, s, me], b_send.at[way, s], b_recv.at[way, s],
-                device_id=(seg, to), device_id_type=MESH,
-            ).start()
-            return carry
-
-        lax.fori_loop(1, PEERS, one, 0)
-        pltpu.make_async_copy(
-            s_b.at[way, s, :, me], r_b.at[way, s, me], b_recv.at[way, s]
+            s_b.at[way, s, q, me], r_b.at[way, s, me, q], b_recv.at[way, s]
         ).start()
 
     def wait_whole(ref, sem):
@@ -228,10 +286,29 @@
 
         shuffle_in(0, s, store)
 
-    def forward(s, carry):
-        take(s, 0)
-        take(s, 1)
-        prepare_in(s)
+    def after_a(s):
+        if s == 0:
+            second(0, 2)
+            third(0, 2)
+            for n in (3, 4):
+                second(0, n)
+                third(0, n)
+            send_weights(1)
+            send_weights(2)
+        final(s, 2)
+        final(s, 3)
+        prepare_mid(s)
+
+    def after_b(s):
+        if s == 0:
+            send_weights(3)
+        final(s, 4)
+        prepare_out(s)
+        final_small(s + 1)
+        final(s + 1, 1)
+        prepare_in(s + 1)
+
+    def forward(s):
         x = xs[s].astype(F32)
         part[0, s] = jnp.sum(x * x, axis=0, keepdims=True)
         send_part(0, s)
@@ -242,43 +319,29 @@
             hn[2 * b + 1] = h[256:]
         shuffle_out(0, s)
         send_a(0, s)
-        take(s, 2)
-        take(s, 3)
-
-        @pl.when(seg == 2 * s + 1)
-        def _():
-            broadcast_weights()
-
-        prepare_mid(s)
-
-        @pl.when(s == SEC - 1)
-        def _():
-            take(s, 4)
+        after_a(s)
+        if s == SEC - 1:
+            final(s, 4)
             start_back(s)
-
         r = lax.rsqrt(wait_part(0, s) / D + epsilon)
         r_s[s] = r
-        wait_whole(r_a.at[0, s], a_recv.at[0, s])
         for q in range(2):
+            wait_whole(r_a.at[0, s, q], a_recv.at[0, s, q])
             v = mm(sel_u[s], r_a[0, s, q].reshape(512, LN)).astype(BF)
             v_n[s, q * 4 : (q + 1) * 4] = v.reshape(4, LN, LN)
-        for c in range(8):
-            u = mm(t_m[s, c], v_n[s, c]) * r
-            value, slope = gelu_pair(u)
-            a = value.astype(BF)
-            u_s[s, c] = u
-            sl[s, c] = slope
-            a_s[s, c] = a
-            zq[c] = mm(t_l[s, c], a).astype(BF)
-        for q in range(2):
+            for c in range(q * 4, q * 4 + 4):
+                u = mm(t_m[s, c], v_n[s, c]) * r
+                value, slope = gelu_pair(u)
+                a = value.astype(BF)
+                u_s[s, c] = u
+                sl[s, c] = slope
+                a_s[s, c] = a
+                zq[c] = mm(t_l[s, c], a).astype(BF)
             z = mm(sel_dt[s], zq[q * 4 : (q + 1) * 4].reshape(512, LN)).astype(BF)
             s_b[0, s, q] = z.reshape(PEERS, 16, LN)
-        send_b(0, s)
-
-        @pl.when(s < SEC - 1)
-        def _():
-            take(s, 4)
-            prepare_out(s)
+            send_b(0, s, q)
+        if s < SEC - 1:
+            after_b(s)
             gather_g(s)
             for b in range(2):
                 y = mm(t_o[s, b], g_n[s, 2 * b : 2 * b + 2].reshape(512, LN))
@@ -286,18 +349,19 @@
                     xs[s, b * LN : (b + 1) * LN].astype(F32) + y
                 ).astype(BF)
 
-        return carry
-
     xs[0] = jnp.transpose(tok[seg].astype(F32)).astype(BF)
     e_c[...] = jnp.transpose(cot[seg].astype(F32))
-    lax.fori_loop(0, SEC, forward, 0)
+    second(0, 1)
+    third(0, 1)
+    final_small(0)
+    final(0, 1)
+    prepare_in(0)
+    for s in range(SEC):
+        forward(s)
 
     grads = (
         (gs_i, gh_i, gr_i), (gs_m, gh_m, gr_m), (gs_l, gh_l, gr_l), (gs_o, gh_o, gr_o)
     )
-
-    def near(s, k):
-        return seg == lax.rem(s + k, SEC)
 
     def ship_half(s, n, k, h):
         src, _, dst = grads[n]
@@ -378,22 +442,23 @@
             combine(s + 1, 1)
 
         r = r_s[s]
-        wait_whole(r_a.at[1, s], a_recv.at[1, s])
+        sum_u[...] = jnp.zeros_like(sum_u)
         for q in range(2):
+            wait_whole(r_a.at[1, s, q], a_recv.at[1, s, q])
             d = mm(sel_d[s], r_a[1, s, q].reshape(512, LN)).astype(BF)
             dz[q * 4 : (q + 1) * 4] = d.reshape(4, LN, LN)
-        sum_u[...] = jnp.zeros_like(sum_u)
-        for c in range(8):
-            d_pre = mm(w_l[s, c], dz[c]) * sl[s, c]
-            sum_u[...] += jnp.sum(d_pre * u_s[s, c], axis=0, keepdims=True)
-            du[c] = (d_pre * r).astype(BF)
-            zq[c] = mm(w_m[s, c], du[c]).astype(BF)
-        part[1, s] = sum_u[...]
-        send_part(1, s)
-        for q in range(2):
+            for c in range(q * 4, q * 4 + 4):
+                d_pre = mm(w_l[s, c], dz[c]) * sl[s, c]
+                sum_u[...] += jnp.sum(d_pre * u_s[s, c], axis=0, keepdims=True)
+                du[c] = (d_pre * r).astype(BF)
+            if q == 1:
+                part[1, s] = sum_u[...]
+                send_part(1, s)
+            for c in range(q * 4, q * 4 + 4):
+                zq[c] = mm(w_m[s, c], du[c]).astype(BF)
             v = mm(sel_ut[s], zq[q * 4 : (q + 1) * 4].reshape(512, LN)).astype(BF)
             s_b[1, s, q] = v.reshape(PEERS, 16, LN)
-        send_b(1, s)
+            send_b(1, s, q)
         for c in range(8):
             emit(o_low, gs_l, (c,), mm_nt(a_s[s, c], dz[c]))
             emit(o_mid, gs_m, (c,), mm_nt(v_n[s, c], du[c]))
@@ -464,12 +529,37 @@
         return carry
 
     lax.fori_loop(0, 2 * SEC, drain, 0)
-    for n, (src, dst) in enumerate(shared):
-        for k in range(SEC - 1) if n == 0 else (0, 2):
-            wait_whole(src, w_send.at[n, k])
-        if n > 0:
+    for k in range(SEC - 1):
+        wait_whole(small, w_send.at[0, k])
+    def passed(*slots):
+        for n in range(1, 5):
+            for slot in slots:
+                wait_whole(half(shared[n][1], 0, slot % 2), w_pass.at[n, slot])
+
+    @pl.when(seg == 0)
+    def _():
+        for n in range(1, 5):
             for h in range(2):
-                wait_whole(half(dst, 0, h), w_pass.at[n, h])
+                wait_whole(half(shared[n][1], 0, h), w_send.at[n, h])
+
+    @pl.when(seg > 0)
+    def _():
+        for n in range(1, 5):
+            for k in range(SEC - 1):
+                wait_whole(shared[n][0], w_send.at[n, k])
+
+    @pl.when(seg == 1)
+    def _():
+        passed(0)
+
+    @pl.when(seg == 2)
+    def _():
+        passed(2, 3)
+
+    @pl.when(seg == 3)
+    def _():
+        passed(1)
+
     for n, (_, mid, landed) in enumerate(grads):
         for h in range(2):
             wait_whole(mid.at[h], h_send.at[n, h])
@@ -513,9 +603,9 @@
         vm((2, 1, 512, LN), BF),
         vm((2, 2, LN, 512), BF), vm((2, 8, LN, LN), BF), vm((2, 8, LN, LN), BF),
         vm((2, 2, 512, LN), BF), vm((3, 1, 256), F32),
-        dma((5, SEC - 1)), dma((SEC, 5)), dma((5, 2)),
+        dma((5, SEC - 1)), dma((SEC, 5, 2)), dma((5, 4)),
         dma((2, SEC)), dma((2, SEC)), dma((2, SEC)),
-        dma((2, SEC)), dma((2, SEC)), dma((2, SEC)),
+        dma((2, SEC, 2)), dma((2, SEC)), dma((2, SEC)),
         dma((2, 4, 2)), dma((2, 4)), dma((4, 2)), dma((2, 4)), dma((SEC,)), dma((3,)),
     ]
     whole = pl.BlockSpec(memory_space=pltpu.VMEM)

time: 219 us -> 192 us (0.88)
  Pallas kernels: 211 us -> 183 us
    pallas_call x1, Pallas kernels: 211 us -> 183 us  [shards(): pl.pallas_call(kernel, out_shape=[jax.ShapeDtypeStruct((2, LN, 512), F32)...]
where the time goes in v3:
time: 192 us
  Pallas kernels  183 us (95%)
  local copies, waits for them, and re-layouts  7.08 us (4%)
    pallas_call x1, Pallas kernels, shards(): pl.pallas_call(kernel, out_shape=[jax.ShapeDtypeStruct((2, LN, 512), F32)...  183 us
    unnamed x19, local copies, waits for them, and re-layouts  7.01 us

profile of v3, /device:TPU:1, one launch (start us, length us, event | category | flops | bytes accessed | tf_op | source)
XLA Modules:
  0.0 191.6 jit_solution(16217609297981280152)
XLA Ops:
  0.6 0.0 copy-start.5
  0.7 0.0 copy-start.6
  0.7 0.1 pad.2.clone
  0.7 0.6 copy-done.5
  1.3 0.0 copy-done.6
  1.3 0.0 copy-start.4
  1.3 0.7 copy-done.4
  2.0 0.7 maximum_maximum_fusion.small
  2.7 183.2 %shard_map.128 = (f32[2,128,512]{2,1,0:T(8,128)}, f32[8,128,128]{2,1,0:T(8,128)}, f32[8,128,128]{2,1,0:T(8,128)}, f32[2,512,128]{2,1,0:T(8,128)}, f32[1,256]{1,0:T(1,128)}) custom-call(bf16[4,128,256]{2,1,0:T(8,128)(2,1)} %tok.1, bf16[4,128,256]{2,1,0:T(8,128)(2,1)} %cot.1, f32[8,256]{1,0:T(8,128)} %maximum_maximum_fusion.small, ...), custom_call_target="tpu_custom_call" | custom-call | tf_op jit(solution)/shard_map/pallas_call | solution.py:612
  185.9 0.0 copy-start.2
  185.9 1.9 %copy.19 = f32[1,2,128,512]{3,2,1,0:T(8,128)} copy(f32[1,2,128,512]{3,2,1,0:T(8,128)} %bitcast.11) | data formatting | bytes 1048576
  187.8 0.0 copy-done.2
  187.8 0.0 copy-start.1
  187.8 0.8 copy.20
  188.6 0.4 copy-done.1
  189.0 0.0 copy-start
  189.0 0.8 copy.21
  189.8 0.4 copy-done
  190.3 0.0 copy-start.3
  190.3 0.8 copy.22
  191.1 0.0 copy-done.3
  191.1 0.6 copy.23
  (2 shorter events, 0.0 us)
Async XLA Ops:
  0.6 0.7 copy-start.5
  0.7 0.7 copy-start.6
  1.3 0.7 copy-start.4
  185.9 1.9 %copy-start.2 = (f32[8,128,128]{2,1,0:T(8,128)S(1)}, f32[8,128,128]{2,1,0:T(8,128)}, u32[]{:S(2)}) copy-start(f32[8,128,128]{2,1,0:T(8,128)} %get-tuple-element.11) | copy-start | bytes 1572868
  187.8 1.2 copy-start.1
  189.0 1.2 copy-start
  190.3 0.8 copy-start.3

commit v4 on v3

--- a/solution.py
+++ b/solution.py
@@ -174,13 +174,15 @@
     perm_t[...] = jnp.where(u256 == (n256 % 4) * 64 + n256 // 4, 1.0, 0.0).astype(BF)
     eye[...] = jnp.where(iota((LN, LN), 0) == iota((LN, LN), 1), 1.0, 0.0).astype(BF)
 
-    def prepare_in(s):
+    def prepare_first(s):
         ident = eye[...]
         for b in range(2):
             for m in range(4):
                 t_i[s, b, m * LN : (m + 1) * LN, :] = mm_nt(
                     ident, w_i[s, b, :, m * LN : (m + 1) * LN]
                 ).astype(BF)
+
+    def prepare_sel(s):
         g_t[s] = jnp.transpose(jnp.broadcast_to(sm[s, 0:1, :], (LN, 256)))
         for which, (sel, sel_t) in enumerate(((sel_u, sel_ut), (sel_d, sel_dt))):
             order_row = sm[s, 1:2, which * LN : (which + 1) * LN].astype(jnp.int32)
@@ -305,13 +307,13 @@
         final(s, 4)
         prepare_out(s)
         final_small(s + 1)
+        prepare_sel(s + 1)
         final(s + 1, 1)
-        prepare_in(s + 1)
+        prepare_first(s + 1)
 
     def forward(s):
         x = xs[s].astype(F32)
         part[0, s] = jnp.sum(x * x, axis=0, keepdims=True)
-        send_part(0, s)
         xg[s] = (x * g_t[s]).astype(BF)
         for b in range(2):
             h = mm(t_i[s, b], xg[s, b * LN : (b + 1) * LN]).astype(BF)
@@ -319,6 +321,7 @@
             hn[2 * b + 1] = h[256:]
         shuffle_out(0, s)
         send_a(0, s)
+        send_part(0, s)
         after_a(s)
         if s == SEC - 1:
             final(s, 4)
@@ -351,11 +354,12 @@
 
     xs[0] = jnp.transpose(tok[seg].astype(F32)).astype(BF)
     e_c[...] = jnp.transpose(cot[seg].astype(F32))
+    final_small(0)
+    prepare_sel(0)
     second(0, 1)
     third(0, 1)
-    final_small(0)
     final(0, 1)
-    prepare_in(0)
+    prepare_first(0)
     for s in range(SEC):
         forward(s)
 
@@ -451,14 +455,13 @@
                 d_pre = mm(w_l[s, c], dz[c]) * sl[s, c]
                 sum_u[...] += jnp.sum(d_pre * u_s[s, c], axis=0, keepdims=True)
                 du[c] = (d_pre * r).astype(BF)
-            if q == 1:
-                part[1, s] = sum_u[...]
-                send_part(1, s)
             for c in range(q * 4, q * 4 + 4):
                 zq[c] = mm(w_m[s, c], du[c]).astype(BF)
             v = mm(sel_ut[s], zq[q * 4 : (q + 1) * 4].reshape(512, LN)).astype(BF)
             s_b[1, s, q] = v.reshape(PEERS, 16, LN)
             send_b(1, s, q)
+        part[1, s] = sum_u[...]
+        send_part(1, s)
         for c in range(8):
             emit(o_low, gs_l, (c,), mm_nt(a_s[s, c], dz[c]))
             emit(o_mid, gs_m, (c,), mm_nt(v_n[s, c], du[c]))
@@ -470,13 +473,13 @@
             combine(s + 1, 0)
 
         combine(s, 3)
-        total = wait_part(1, s)
         wait_whole(r_b.at[1, s], b_recv.at[1, s])
 
         def store(l, m, value):
             hn[l, m * 64 : (m + 1) * 64, :] = value
 
         shuffle_in(1, s, store)
+        total = wait_part(1, s)
         scale = r * r * total / D
         for b in range(2):
             lo = b * LN

time: 192 us -> 192 us (level)
  no operation moved by 1% of the time
where the time goes in v4:
time: 192 us
  Pallas kernels  183 us (95%)
  local copies, waits for them, and re-layouts  7.08 us (4%)
    pallas_call x1, Pallas kernels, shards(): pl.pallas_call(kernel, out_shape=[jax.ShapeDtypeStruct((2, LN, 512), F32)...  183 us
    unnamed x19, local copies, waits for them, and re-layouts  7.01 us

profile of v4, /device:TPU:1, one launch (start us, length us, event | category | flops | bytes accessed | tf_op | source)
XLA Modules:
  0.0 191.8 jit_solution(6154748713597441626)
XLA Ops:
  0.6 0.0 copy-start.5
  0.7 0.0 copy-start.6
  0.7 0.1 pad.2.clone
  0.7 0.6 copy-done.5
  1.3 0.0 copy-done.6
  1.3 0.0 copy-start.4
  1.3 0.7 copy-done.4
  2.0 0.7 maximum_maximum_fusion.small
  2.7 183.3 %shard_map.128 = (f32[2,128,512]{2,1,0:T(8,128)}, f32[8,128,128]{2,1,0:T(8,128)}, f32[8,128,128]{2,1,0:T(8,128)}, f32[2,512,128]{2,1,0:T(8,128)}, f32[1,256]{1,0:T(1,128)}) custom-call(bf16[4,128,256]{2,1,0:T(8,128)(2,1)} %tok.1, bf16[4,128,256]{2,1,0:T(8,128)(2,1)} %cot.1, f32[8,256]{1,0:T(8,128)} %maximum_maximum_fusion.small, ...), custom_call_target="tpu_custom_call" | custom-call | tf_op jit(solution)/shard_map/pallas_call | solution.py:615
  186.0 0.0 copy-start.2
  186.0 1.9 %copy.19 = f32[1,2,128,512]{3,2,1,0:T(8,128)} copy(f32[1,2,128,512]{3,2,1,0:T(8,128)} %bitcast.11) | data formatting | bytes 1048576
  187.9 0.0 copy-done.2
  187.9 0.0 copy-start.1
  187.9 0.8 copy.20
  188.7 0.4 copy-done.1
  189.2 0.0 copy-start
  189.2 0.8 copy.21
  190.0 0.4 copy-done
  190.4 0.0 copy-start.3
  190.4 0.8 copy.22
  191.2 0.0 copy-done.3
  191.2 0.6 copy.23
  (2 shorter events, 0.0 us)
Async XLA Ops:
  0.6 0.7 copy-start.5
  0.7 0.7 copy-start.6
  1.3 0.7 copy-start.4
  186.0 1.9 %copy-start.2 = (f32[8,128,128]{2,1,0:T(8,128)S(1)}, f32[8,128,128]{2,1,0:T(8,128)}, u32[]{:S(2)}) copy-start(f32[8,128,128]{2,1,0:T(8,128)} %get-tuple-element.11) | copy-start | bytes 1572868
  187.9 1.2 copy-start.1
  189.2 1.2 copy-start
  190.4 0.8 copy-start.3

commit v5 on v3

--- a/solution.py
+++ b/solution.py
@@ -215,7 +215,7 @@
             ).start()
             return carry
 
-        lax.fori_loop(0, PEERS - 1, one, 0)
+        lax.fori_loop(0, PEERS - 1, one, 0, unroll=PEERS - 1 if way == 1 else 1)
         pltpu.make_async_copy(part.at[way, s], parts.at[way, s, me], p_recv.at[way, s]).start()
 
     def wait_part(way, s):
@@ -234,7 +234,7 @@
                 ).start()
                 return carry
 
-            lax.fori_loop(0, PEERS - 1, one, 0)
+            lax.fori_loop(0, PEERS - 1, one, 0, unroll=PEERS - 1 if way == 1 else 1)
             pltpu.make_async_copy(
                 s_a.at[way, s, me, q], r_a.at[way, s, q, me], a_recv.at[way, s, q]
             ).start()
@@ -248,7 +248,7 @@
             ).start()
             return carry
 
-        lax.fori_loop(0, PEERS - 1, one, 0)
+        lax.fori_loop(0, PEERS - 1, one, 0, unroll=PEERS - 1 if way == 1 else 1)
         pltpu.make_async_copy(
             s_b.at[way, s, q, me], r_b.at[way, s, me, q], b_recv.at[way, s]
         ).start()

time: 192 us -> 189 us (0.984)
  Pallas kernels: 183 us -> 181 us
    pallas_call x1, Pallas kernels: 183 us -> 181 us  [shards(): pl.pallas_call(kernel, out_shape=[jax.ShapeDtypeStruct((2, LN, 512), F32)...]
where the time goes in v5:
time: 189 us
  Pallas kernels  181 us (96%)
  local copies, waits for them, and re-layouts  7.08 us (4%)
    pallas_call x1, Pallas kernels, shards(): pl.pallas_call(kernel, out_shape=[jax.ShapeDtypeStruct((2, LN, 512), F32)...  181 us
    unnamed x19, local copies, waits for them, and re-layouts  7.01 us

profile of v5, /device:TPU:1, one launch (start us, length us, event | category | flops | bytes accessed | tf_op | source)
XLA Modules:
  0.0 189.2 jit_solution(8743432167531832004)
XLA Ops:
  0.6 0.0 copy-start.5
  0.7 0.0 copy-start.6
  0.7 0.1 pad.2.clone
  0.7 0.6 copy-done.5
  1.3 0.0 copy-done.6
  1.3 0.0 copy-start.4
  1.3 0.7 copy-done.4
  2.0 0.7 maximum_maximum_fusion.small
  2.7 180.8 %shard_map.128 = (f32[2,128,512]{2,1,0:T(8,128)}, f32[8,128,128]{2,1,0:T(8,128)}, f32[8,128,128]{2,1,0:T(8,128)}, f32[2,512,128]{2,1,0:T(8,128)}, f32[1,256]{1,0:T(1,128)}) custom-call(bf16[4,128,256]{2,1,0:T(8,128)(2,1)} %tok.1, bf16[4,128,256]{2,1,0:T(8,128)(2,1)} %cot.1, f32[8,256]{1,0:T(8,128)} %maximum_maximum_fusion.small, ...), custom_call_target="tpu_custom_call" | custom-call | tf_op jit(solution)/shard_map/pallas_call | solution.py:612
  183.4 0.0 copy-start.2
  183.4 1.9 %copy.19 = f32[1,2,128,512]{3,2,1,0:T(8,128)} copy(f32[1,2,128,512]{3,2,1,0:T(8,128)} %bitcast.11) | data formatting | bytes 1048576
  185.4 0.0 copy-done.2
  185.4 0.0 copy-start.1
  185.4 0.8 copy.20
  186.2 0.4 copy-done.1
  186.6 0.0 copy-start
  186.6 0.8 copy.21
  187.4 0.4 copy-done
  187.8 0.0 copy-start.3
  187.8 0.8 copy.22
  188.6 0.0 copy-done.3
  188.6 0.6 copy.23
  (2 shorter events, 0.0 us)
Async XLA Ops:
  0.6 0.7 copy-start.5
  0.7 0.7 copy-start.6
  1.3 0.7 copy-start.4
  183.4 1.9 %copy-start.2 = (f32[8,128,128]{2,1,0:T(8,128)S(1)}, f32[8,128,128]{2,1,0:T(8,128)}, u32[]{:S(2)}) copy-start(f32[8,128,128]{2,1,0:T(8,128)} %get-tuple-element.11) | copy-start | bytes 1572868
  185.4 1.2 copy-start.1
  186.6 1.2 copy-start
  187.8 0.8 copy-start.3
